TPU v7x, 32 devices: a whole 2x2x4 slice. The times are simulated.
32 devices in a mesh: gx: 4 (over x, core), gy: 8 (over z, y).
Axes of the slice: x: 2, y: 2, z: 4, core: 2. Of those that a mesh axis runs over, the one named last changes fastest.
Arguments:
- reference_image: bfloat16 [32, 128, 1024], P(None, 'gx', 'gy'), may hold values from -6 to 6
- moving_image: float32 [44, 128, 1024], P(None, 'gx', 'gy'), may hold values from -6 to 6
- image_gradient: bfloat16 [3, 32, 128, 1024], P(None, None, 'gx', 'gy'), may hold values from -1.5 to 1.5
- voxel_shift: int32 [3, 4, 16, 128], P(None, None, 'gx', 'gy'), may hold values from -6 to 5
- subvoxel: float32 [3, 4, 16, 128], P(None, None, 'gx', 'gy'), may hold values from 0 to 1
Outputs:
- increment: float32 [3, 5, 16, 128], P(None, None, 'gx', 'gy')
- cg_residual: float32 [3, 5, 16, 128], P(None, None, 'gx', 'gy')
All inputs are finite; a program needn't handle non-finite values.
Results may differ from a plain program's by a relative error of at most 0.0003.
Values sent between devices are 32-bit elements; how exact they have to be, the bound alone decides.
A program may use at most 128 MiB of HBM per device.

v0:
```python
import jax
import jax.numpy as jnp
import numpy as np
from jax import lax
from jax.sharding import PartitionSpec as P

ELEM = 8
HW = 6
ITERS = 3


ridge_weight = 2.0


def padded_2(cells, sides, width):
    for axis, dim in sides:
        count = lax.axis_size(axis)
        ends = count - 1
        head = lax.slice_in_dim(cells, 0, width, axis=dim)
        tail = lax.slice_in_dim(cells, cells.shape[dim] - width, cells.shape[dim], axis=dim)
        cells = jnp.concatenate(
            [
                lax.ppermute(tail, axis, [(i, (i + 1) % count) for i in range(ends)]),
                cells,
                lax.ppermute(head, axis, [((i + 1) % count, i) for i in range(ends)]),
            ],
            axis=dim,
        )
    return cells


def linear_basis():
    centres = (jnp.arange(ELEM, dtype=jnp.float32) + 0.5) / ELEM
    return jnp.stack([1.0 - centres, centres])


def corner_weights():
    shape_basis = linear_basis()
    return jnp.einsum("pi,qj,rl->pqrijl", shape_basis, shape_basis, shape_basis).reshape(
        8, ELEM * ELEM * ELEM
    )


def corner_sides():
    return [(side_z, side_x, side_y) for side_z in (0, 1) for side_x in (0, 1) for side_y in (0, 1)]


def element_major(volume, count_z, count_x, count_y):
    shaped = volume.reshape(count_z, ELEM, count_x, ELEM, count_y, ELEM)
    return shaped.transpose(1, 3, 5, 0, 2, 4).reshape(
        ELEM * ELEM * ELEM, count_z * count_x * count_y
    )


def element_stiffness(gradient_cols):
    weights = corner_weights()
    pair_weights = (weights[:, None, :] * weights[None, :, :]).reshape(64, ELEM * ELEM * ELEM)
    blocks = {}
    for first_comp in range(3):
        for second_comp in range(first_comp, 3):
            product = gradient_cols[first_comp] * gradient_cols[second_comp]
            summed = jnp.dot(pair_weights, product, precision=lax.Precision.HIGHEST)
            blocks[first_comp, second_comp] = summed.reshape(8, 8, -1)
            blocks[second_comp, first_comp] = blocks[first_comp, second_comp]
    stiff_rows = []
    for first_comp in range(3):
        stiff_rows.append(
            jnp.stack([blocks[first_comp, second_comp] for second_comp in range(3)], axis=2)
        )
    return jnp.stack(stiff_rows, axis=1)


def element_load(image_cols, gradient_cols, warped):
    weights = corner_weights()
    mismatch = image_cols - warped
    load_terms = [
        jnp.dot(weights, gradient_cols[component] * mismatch, precision=lax.Precision.HIGHEST)
        for component in range(3)
    ]
    return jnp.stack(load_terms, axis=1)


def warp_columns(source, start_z, start_x, start_y, weight_z, weight_x, weight_y):

    def cut_block(corner_z, corner_x, corner_y):
        return lax.dynamic_slice(
            source, (corner_z, corner_x, corner_y), (ELEM + 1, ELEM + 1, ELEM + 1)
        )

    gathered = jax.vmap(cut_block, out_axes=3)(start_z, start_x, start_y)
    along_z = (1.0 - weight_z) * gathered[:ELEM] + weight_z * gathered[1:]
    along_x = (1.0 - weight_x) * along_z[:, :ELEM] + weight_x * along_z[:, 1:]
    along_y = (1.0 - weight_y) * along_x[:, :, :ELEM] + weight_y * along_x[:, :, 1:]
    return along_y.reshape(ELEM * ELEM * ELEM, -1)


def nodes_to_elements(nodal_field, count_z, count_x, count_y):
    picked = [
        nodal_field[
            :, side_z : side_z + count_z, side_x : side_x + count_x, side_y : side_y + count_y
        ]
        for side_z, side_x, side_y in corner_sides()
    ]
    return jnp.stack(picked).reshape(8, 3, -1)


def elements_to_nodes(element_terms, count_z, count_x, count_y):
    shaped = element_terms.reshape(8, 3, count_z, count_x, count_y)
    nodal_sum = jnp.zeros((3, count_z + 1, count_x + 1, count_y + 1), jnp.float32)
    for corner_index, (side_z, side_x, side_y) in enumerate(corner_sides()):
        nodal_sum = nodal_sum + jnp.pad(
            shaped[corner_index],
            ((0, 0), (side_z, 1 - side_z), (side_x, 1 - side_x), (side_y, 1 - side_y)),
        )
    return nodal_sum


def element_product(stiffness, element_values):
    return jnp.sum(stiffness * element_values[None, None], axis=(2, 3))


def fold_rims(extended, fold_dim):
    size_along = extended.shape[fold_dim]
    lower_rim = lax.slice_in_dim(extended, 0, 1, axis=fold_dim)
    upper_rim = lax.slice_in_dim(extended, size_along - 1, size_along, axis=fold_dim)
    core_rows = lax.slice_in_dim(extended, 1, size_along - 1, axis=fold_dim)
    first_row = lax.slice_in_dim(core_rows, 0, 1, axis=fold_dim) + lower_rim
    last_row = (
        lax.slice_in_dim(core_rows, size_along - 3, size_along - 2, axis=fold_dim) + upper_rim
    )
    middle = lax.slice_in_dim(core_rows, 1, size_along - 3, axis=fold_dim)
    return jnp.concatenate([first_row, middle, last_row], axis=fold_dim)


def face_sum(nodal_field):
    extended = padded_2(nodal_field, (("gx", 2), ("gy", 3)), 1)
    return fold_rims(fold_rims(extended, 2), 3)


def squares(owner_weight, residual):
    return lax.psum(jnp.sum(residual * residual * owner_weight), ("gx", "gy"))


def is_inner(column, count_x, count_y):
    along_x = column // count_y % count_x
    along_y = column % count_y
    return 1 <= along_x <= count_x - 2 and 1 <= along_y <= count_y - 2


def body(reference_image, moving_image, image_gradient, voxel_shift, subvoxel):
    count_z = voxel_shift.shape[1]
    count_x = voxel_shift.shape[2]
    count_y = voxel_shift.shape[3]
    plane = count_x * count_y
    padded = padded_2(moving_image, (("gx", 1), ("gy", 2)), HW)
    gradient_cols = [
        element_major(image_gradient[component], count_z, count_x, count_y).astype(jnp.float32)
        for component in range(3)
    ]
    image_cols = element_major(reference_image, count_z, count_x, count_y).astype(jnp.float32)
    stiffness = element_stiffness(gradient_cols)
    flat_index = jnp.arange(count_z * plane, dtype=jnp.int32)
    elem_z = flat_index // plane
    elem_x = flat_index // count_y % count_x
    elem_y = flat_index % count_y
    start_z = elem_z * ELEM + voxel_shift[0].reshape(-1) + HW
    start_x = elem_x * ELEM + voxel_shift[1].reshape(-1) + HW
    start_y = elem_y * ELEM + voxel_shift[2].reshape(-1) + HW
    weight_z = subvoxel[0].reshape(-1)
    weight_x = subvoxel[1].reshape(-1)
    weight_y = subvoxel[2].reshape(-1)
    total_cols = count_z * plane
    inner_list = [column for column in range(total_cols) if is_inner(column, count_x, count_y)]
    outer_list = [column for column in range(total_cols) if not is_inner(column, count_x, count_y)]
    inner_cols = np.array(inner_list, dtype=np.int32)
    outer_cols = np.array(outer_list, dtype=np.int32)
    local_pad = jnp.pad(moving_image, ((0, 0), (HW, HW), (HW, HW)))
    inner_part = warp_columns(
        local_pad,
        start_z[inner_cols],
        start_x[inner_cols],
        start_y[inner_cols],
        weight_z[inner_cols],
        weight_x[inner_cols],
        weight_y[inner_cols],
    )
    outer_part = warp_columns(
        padded,
        start_z[outer_cols],
        start_x[outer_cols],
        start_y[outer_cols],
        weight_z[outer_cols],
        weight_x[outer_cols],
        weight_y[outer_cols],
    )
    warped = jnp.zeros((ELEM * ELEM * ELEM, count_z * plane), jnp.float32)
    warped = warped.at[:, inner_cols].set(inner_part).at[:, outer_cols].set(outer_part)
    load_flat = element_load(image_cols, gradient_cols, warped)
    load_nodes = face_sum(elements_to_nodes(load_flat, count_z, count_x, count_y))
    last_x = (lax.axis_index("gx") == lax.axis_size("gx") - 1).astype(jnp.float32)
    last_y = (lax.axis_index("gy") == lax.axis_size("gy") - 1).astype(jnp.float32)
    row_weight = jnp.concatenate([jnp.ones((count_x,), jnp.float32), last_x[None]])
    col_weight = jnp.concatenate([jnp.ones((count_y,), jnp.float32), last_y[None]])
    owner_weight = row_weight[:, None] * col_weight[None, :]
    solution = jnp.zeros_like(load_nodes)
    residual = load_nodes
    direction = load_nodes
    norm_now = squares(owner_weight, residual)
    for iteration in range(ITERS):
        element_values = nodes_to_elements(direction, count_z, count_x, count_y)
        partial_nodes = elements_to_nodes(
            element_product(stiffness, element_values), count_z, count_x, count_y
        )
        image_dir = face_sum(partial_nodes) + ridge_weight * direction
        step_length = norm_now / lax.psum(
            jnp.sum(direction * image_dir * owner_weight), ("gx", "gy")
        )
        solution = solution + step_length * direction
        residual = residual - step_length * image_dir
        norm_next = squares(owner_weight, residual)
        direction = residual + norm_next / norm_now * direction
        norm_now = norm_next
    return (solution[:, :, :count_x, :count_y], residual[:, :, :count_x, :count_y])


def solution(mesh):
    placed = (
        P(None, "gx", "gy"),
        P(None, "gx", "gy"),
        P(None, None, "gx", "gy"),
        P(None, None, "gx", "gy"),
        P(None, None, "gx", "gy"),
    )
    return jax.shard_map(
        body,
        mesh=mesh,
        in_specs=placed,
        out_specs=(P(None, None, "gx", "gy"), P(None, None, "gx", "gy")),
        check_vma=False,
    )
```

profile of v0, /device:TPU:0, one launch (start us, length us, event | category | flops | bytes accessed | tf_op | source)
XLA Modules:
  0.0 1521.6 jit_solution(5182805776762409984)
XLA Ops:
  27.3 6.1 reshape.381
  33.5 7.8 copy.135
  41.3 5.3 reshape.377
  46.6 6.1 reshape.383
  52.7 7.8 copy.149
  60.6 5.3 reshape.379
  65.8 6.1 reshape.384
  72.0 7.8 copy.151
  79.8 5.5 reshape.380
  93.6 450.7 %while.2 = (s32[]{:T(128)}, f32[44,44,140]{2,1,0:T(8,128)}, s32[112,3]{0,1:T(4,128)S(1)}, f32[112,9,9,9]{3,2,1,0:T(8,128)}, s32[]{:T(128)}) while((s32[]{:T(128)}, f32[44,44,140]{2,1,0:T(8,128)}, s32[112,3]{0,1:T(4,128)S(1)}, f32[112,9,9,9]{3,2,1,0:T(8,128)}, s32[]{:T(128)}) %tuple.123), condition=%wide.while_cond, body=%wide.while_body.sunk | while | flops 2 | bytes 149617 | solution.py:86
  94.2 3.4 bitcast_dynamic-update-slice_fusion.4
  106.3 3.4 bitcast_dynamic-update-slice_fusion.4
  126.4 3.4 bitcast_dynamic-update-slice_fusion.4
  130.4 3.4 bitcast_dynamic-update-slice_fusion.4
  146.5 3.4 bitcast_dynamic-update-slice_fusion.4
  166.7 3.4 bitcast_dynamic-update-slice_fusion.4
  174.7 3.4 bitcast_dynamic-update-slice_fusion.4
  198.8 3.4 bitcast_dynamic-update-slice_fusion.4
  210.9 3.4 bitcast_dynamic-update-slice_fusion.4
  214.9 3.4 bitcast_dynamic-update-slice_fusion.4
  227.0 3.4 bitcast_dynamic-update-slice_fusion.4
  231.1 3.4 bitcast_dynamic-update-slice_fusion.4
  247.2 3.4 bitcast_dynamic-update-slice_fusion.4
  259.2 3.4 bitcast_dynamic-update-slice_fusion.4
  287.4 3.4 bitcast_dynamic-update-slice_fusion.4
  295.4 3.4 bitcast_dynamic-update-slice_fusion.4
  319.6 3.4 bitcast_dynamic-update-slice_fusion.4
  323.6 3.4 bitcast_dynamic-update-slice_fusion.4
  335.6 3.4 bitcast_dynamic-update-slice_fusion.4
  343.7 3.4 bitcast_dynamic-update-slice_fusion.4
  351.8 3.4 bitcast_dynamic-update-slice_fusion.4
  359.8 3.4 bitcast_dynamic-update-slice_fusion.4
  367.9 3.4 bitcast_dynamic-update-slice_fusion.4
  375.9 3.4 bitcast_dynamic-update-slice_fusion.4
  392.0 3.4 bitcast_dynamic-update-slice_fusion.4
  404.1 3.4 bitcast_dynamic-update-slice_fusion.4
  408.1 3.4 bitcast_dynamic-update-slice_fusion.4
  420.2 3.4 bitcast_dynamic-update-slice_fusion.4
  432.3 3.4 bitcast_dynamic-update-slice_fusion.4
  444.4 3.4 bitcast_dynamic-update-slice_fusion.4
  468.5 3.4 bitcast_dynamic-update-slice_fusion.4
  480.6 3.4 bitcast_dynamic-update-slice_fusion.4
  544.3 4.8 copy.137
  563.3 4.4 collective-permute-start.2
  576.6 6.2 reshape.382
  582.7 7.8 copy.136
  590.6 5.3 reshape.378
  596.0 7.3 pad_maximum_fusion
  603.4 608.5 %while.3 = (s32[]{:T(128)}, f32[44,44,140]{1,0,2:T(8,128)}, s32[144,3]{0,1:T(4,128)S(1)}, f32[144,9,9,9]{3,2,1,0:T(8,128)}, s32[]{:T(128)}) while((s32[]{:T(128)}, f32[44,44,140]{1,0,2:T(8,128)}, s32[144,3]{0,1:T(4,128)S(1)}, f32[144,9,9,9]{3,2,1,0:T(8,128)}, s32[]{:T(128)}) %tuple.126), condition=%wide.while_cond.1, body=%wide.while_body.1.sunk | while | flops 2 | bytes 88937 | solution.py:86
  1211.9 8.2 copy.145
  1235.0 4.6 collective-permute-start.6
  1241.4 4.7 collective-permute-done.7
  1256.0 4.8 collective-permute-start.10
  1262.7 4.3 collective-permute-done.11
  1268.5 40.9 %all-reduce.35 = (f32[]{:T(128)}, f32[]{:T(128)}) all-reduce(f32[]{:T(128)} %get-tuple-element.31, f32[]{:T(128)} %get-tuple-element.30), channel_id=1, replica_groups=mesh['gx'=4,'gy'=8] {'gx','gy'}, use_global_device_ids=true, to_apply=%region_3.4 | all-reduce | flops 2 | bytes 16 | tf_op jit(solution)/shard_map/psum | solution.py:141
  1311.4 39.8 %psum.44 = f32[]{:T(128)} all-reduce(f32[]{:T(128)} %multiply_reduce_fusion.6), channel_id=1, replica_groups=mesh['gx'=4,'gy'=8] {'gx','gy'}, use_global_device_ids=true, to_apply=%region_8.9 | all-reduce | flops 1 | bytes 8 | tf_op jit(solution)/shard_map/psum | solution.py:141
  1357.1 4.3 collective-permute-done.13
  1366.4 4.3 collective-permute-done.15
  1372.3 42.5 %psum.45 = f32[]{:T(128)} all-reduce(f32[]{:T(128)} %multiply_reduce_fusion.5), channel_id=1, replica_groups=mesh['gx'=4,'gy'=8] {'gx','gy'}, use_global_device_ids=true, to_apply=%region_11.12 | all-reduce | flops 1 | bytes 8 | tf_op jit(solution)/shard_map/psum | solution.py:215
  1416.8 39.1 %psum.46 = f32[]{:T(128)} all-reduce(f32[]{:T(128)} %get-tuple-element.84), channel_id=1, replica_groups=mesh['gx'=4,'gy'=8] {'gx','gy'}, use_global_device_ids=true, to_apply=%region_13.14 | all-reduce | flops 1 | bytes 8 | tf_op jit(solution)/shard_map/psum | solution.py:141
  1461.9 4.3 collective-permute-done.17
  1466.3 4.0 collective-permute-start.18
  1472.1 4.3 collective-permute-done.19
  1477.9 40.6 %psum.47 = f32[]{:T(128)} all-reduce(f32[]{:T(128)} %get-tuple-element.82), channel_id=1, replica_groups=mesh['gx'=4,'gy'=8] {'gx','gy'}, use_global_device_ids=true, to_apply=%region_16.17 | all-reduce | flops 1 | bytes 8 | tf_op jit(solution)/shard_map/psum | solution.py:215
  (1338 shorter events, 1058.0 us)
Async XLA Ops:
  0.6 17.1 %copy-start.14 = (f32[3,4,4,16]{3,2,1,0:T(4,128)S(1)}, f32[3,4,4,16]{3,2,1,0:T(4,128)}, u32[]{:S(2)}) copy-start(f32[3,4,4,16]{3,2,1,0:T(4,128)} %param.25) | copy-start | bytes 9220
  2.4 552.7 %collective-permute-start = (f32[44,6,128]{2,0,1:T(8,128)}, f32[44,6,128]{2,0,1:T(8,128)}, u32[]{:S(2)}, u32[]{:S(2)}) collective-permute-start(f32[44,6,128]{2,0,1:T(8,128)} %copy.157), channel_id=1, source_target_pairs={{0,8},{8,16},{16,24},{1,9},{9,17},{17,25},{2,10},{10,18},{18,26},{... | collective-permute-start | bytes 405512 | tf_op jit(solution)/shard_map/ppermute | solution.py:23
  6.1 552.1 %collective-permute-start.1 = (f32[44,6,128]{2,0,1:T(8,128)}, f32[44,6,128]{2,0,1:T(8,128)}, u32[]{:S(2)}, u32[]{:S(2)}) collective-permute-start(f32[44,6,128]{2,0,1:T(8,128)} %copy.158), channel_id=1, source_target_pairs={{8,0},{16,8},{24,16},{9,1},{17,9},{25,17},{10,2},{18,10},{26,18},{... | collective-permute-start | bytes 405512 | tf_op jit(solution)/shard_map/ppermute | solution.py:25
  14.9 12.3 copy-start.8
  19.5 70.4 %copy-start.15 = (f32[144]{0:T(256)}, f32[144]{0:T(256)S(1)}, u32[]{:S(2)}) copy-start(f32[144]{0:T(256)S(1)} %gather_fusion.8) | copy-start | bytes 1732
  22.5 68.0 %copy-start.17 = (f32[144]{0:T(256)}, f32[144]{0:T(256)S(1)}, u32[]{:S(2)}) copy-start(f32[144]{0:T(256)S(1)} %gather_fusion.7) | copy-start | bytes 1732
  25.5 65.6 %copy-start.19 = (f32[144]{0:T(256)}, f32[144]{0:T(256)S(1)}, u32[]{:S(2)}) copy-start(f32[144]{0:T(256)S(1)} %gather_fusion.6) | copy-start | bytes 1732
  46.6 39.5 %copy-start.1 = (f32[512,256]{1,0:T(8,128)}, f32[512,256]{1,0:T(8,128)S(1)}, u32[]{:S(2)}) copy-start(f32[512,256]{1,0:T(8,128)S(1)} %reshape.377) | copy-start | bytes 1572868
  65.8 483.5 %copy-start.2 = (f32[512,256]{1,0:T(8,128)}, f32[512,256]{1,0:T(8,128)S(1)}, u32[]{:S(2)}) copy-start(f32[512,256]{1,0:T(8,128)S(1)} %reshape.379) | copy-start | bytes 1572868
  79.8 11.8 copy-start.4
  85.3 8.3 copy-start.3
  552.6 8.7 copy-start
  561.2 7.8 copy-start.25
  561.3 7.8 copy-start.26
  561.3 7.8 copy-start.27
  563.3 13.2 copy-start.9
  563.3 32.7 %collective-permute-start.2 = (f32[44,44,6]{1,0,2:T(8,128)}, f32[44,44,6]{1,0,2:T(8,128)S(1)}, u32[]{:S(2)}, u32[]{:S(2)}) collective-permute-start(f32[44,44,6]{1,0,2:T(8,128)} %get-tuple-element.94), channel_id=1, source_target_pairs={{0,1},{1,2},{2,3},{3,4},{4,5},{5,6},{6,7},{8,9},{9,10},{10,11},{11... | collective-permute-start | bytes 139400 | tf_op jit(solution)/shard_map/ppermute | solution.py:23
  567.7 28.3 %collective-permute-start.3 = (f32[44,44,6]{1,0,2:T(8,128)}, f32[44,44,6]{1,0,2:T(8,128)S(1)}, u32[]{:S(2)}, u32[]{:S(2)}) collective-permute-start(f32[44,44,6]{1,0,2:T(8,128)} %get-tuple-element.95), channel_id=1, source_target_pairs={{1,0},{2,1},{3,2},{4,3},{5,4},{6,5},{7,6},{9,8},{10,9},{11,10},{12... | collective-permute-start | bytes 139400 | tf_op jit(solution)/shard_map/ppermute | solution.py:25
  1211.9 8.2 copy-start.16
  1211.9 8.2 copy-start.24
  1220.1 0.7 copy-start.18
  1220.1 0.7 copy-start.23
  1220.1 0.8 copy-start.20
  1220.1 0.8 copy-start.22
  1220.7 2.2 copy-start.21
  1223.0 1.3 copy-start.6
  1223.0 1.9 copy-start.7
  1224.3 1.1 copy-start.5
  1224.3 7.3 copy-start.10
  1224.3 7.3 copy-start.11
  1224.3 7.3 copy-start.12
  1224.4 7.3 copy-start.13
  1226.9 4.8 collective-permute-start.4
  1230.3 4.5 collective-permute-start.5
  1235.0 6.4 collective-permute-start.6
  1239.5 6.6 collective-permute-start.7
  1249.0 4.5 collective-permute-start.8
  1252.2 3.8 collective-permute-start.9
  1256.0 6.7 collective-permute-start.10
  1260.9 6.1 collective-permute-start.11
  1354.5 2.6 collective-permute-start.12
  1355.8 5.6 collective-permute-start.13
  1361.5 4.9 collective-permute-start.14
  1364.6 6.2 collective-permute-start.15
  1459.3 2.6 collective-permute-start.16
  1460.6 5.6 collective-permute-start.17
  1466.3 5.9 collective-permute-start.18
  1470.3 6.1 collective-permute-start.19
where the time goes:
time: 1550 us; the launch traced here: 1520 us
  local copies, waits for them, and re-layouts  1200 us (77%)
  blocking collectives  203 us (13%)
  starting transfers between devices  46.1 us (3%)
  waiting for transfers between devices  33.4 us (2%)
  other arithmetic  24.1 us (2%)
    gather x1056, local copies, waits for them, and re-layouts  1060 us
    psum x3, blocking collectives, squares(): return lax.psum(jnp.sum(residual * residual * owner_weight), ('gx', 'gy'))  120 us
    psum x2, blocking collectives, body(): lax.psum(jnp.sum(direction * image_dir * owner_weight), ('gx', 'gy'))  83.1 us
    convert_element_type x12, local copies, waits for them, and re-layouts, body(): element_major(image_gradient[component], count_z, count_x, count_y)  64.1 us
    ppermute x10, starting transfers between devices, padded_2(): lax.ppermute(tail, axis, [(i, (i + 1) % count) for i in range(ends)])  32.9 us
    ppermute x10, waiting for transfers between devices, padded_2(): lax.ppermute(head, axis, [((i + 1) % count, i) for i in range(ends)])  31.6 us
  transfers between devices with their start and end apart: 20, of which 12 were waited for; matrix products, arithmetic and copies ran while one was open for 38% of the time, Pallas kernels for 0%

commit v1 on v0

v1 whole, which is shorter than its diff:
```python
import functools

import jax
import jax.numpy as jnp
import numpy as np
from jax import lax
from jax.experimental import pallas as pl
from jax.experimental.pallas import tpu as pltpu
from jax.sharding import PartitionSpec as P

ELEM = 8
HW = 6
ITERS = 3
LANES = 128
ROWS = 8
RIDGE = 2.0
TAPS = 2 * HW + 1
COMP = {(0, 0): 0, (0, 1): 1, (0, 2): 2, (1, 1): 3, (1, 2): 4, (2, 2): 5}
MESH = pl.DeviceIdType.MESH


def phi():
    centre = (np.arange(ELEM, dtype=np.float64) + 0.5) / ELEM
    return np.stack([1.0 - centre, centre])


def placed_weights(classes, count_x, count_y, stride):
    size_y = count_y * ELEM
    out = np.zeros((count_x, size_y, len(classes), LANES), np.float32)
    for ex in range(count_x):
        for y in range(size_y):
            for c, w in enumerate(classes):
                out[ex, y, c, ex * stride + y // ELEM] = w[y % ELEM]
    return out.reshape(count_x * size_y, len(classes) * LANES)


def exact_dot(values, weights):
    total = None
    rest = values
    for _ in range(3):
        part = rest.astype(jnp.bfloat16)
        rest = rest - part.astype(jnp.float32)
        term = jnp.dot(part, weights, preferred_element_type=jnp.float32)
        total = term if total is None else total + term
    return total


def padded_2(cells, sides, width):
    for axis, dim in sides:
        count = lax.axis_size(axis)
        ends = count - 1
        head = lax.slice_in_dim(cells, 0, width, axis=dim)
        tail = lax.slice_in_dim(cells, cells.shape[dim] - width, cells.shape[dim], axis=dim)
        cells = jnp.concatenate(
            [
                lax.ppermute(tail, axis, [(i, (i + 1) % count) for i in range(ends)]),
                cells,
                lax.ppermute(head, axis, [((i + 1) % count, i) for i in range(ends)]),
            ],
            axis=dim,
        )
    return cells


def element_kernel(dims, pad_ref, image_ref, grad_ref, shift_ref, frac_ref, wx_ref, bs_ref, bl_ref,
                   stiff_ref, load_ref, rolled, ysum, xsum, vs, vl):
    count_z, count_x, size_y = dims
    p = phi()
    pairs = [p[0] * p[0], p[0] * p[1], p[1] * p[1]]
    span = ELEM + TAPS - 1
    depth = pad_ref.shape[0]
    f32 = jnp.float32

    @pl.loop(0, depth)
    def _(z):
        row = pad_ref[z]
        for d in range(TAPS):
            rolled[d, z] = row[:, d : d + size_y]

    vs[...] = jnp.zeros_like(vs)
    vl[...] = jnp.zeros_like(vl)

    def taps(axis, row):
        s = shift_ref[axis, pl.ds(row, 1), :] + HW
        w = frac_ref[axis, pl.ds(row, 1), :]
        zero = jnp.zeros_like(w)
        return [
            jnp.where(s == d, 1.0 - w, zero) + jnp.where(s == d - 1, w, zero) for d in range(TAPS)
        ]

    for ez in range(count_z):

        @pl.loop(0, count_x)
        def _(ex, ez=ez):
            row = ez * count_x + ex
            z0 = ez * ELEM
            x0 = pl.multiple_of(ex * ELEM, ELEM)
            chunk = 4
            wy = [jnp.broadcast_to(t, (ELEM, size_y)) for t in taps(2, row)]
            for c in range(0, span, chunk):
                for t in range(3):
                    acc = None
                    for d in range(TAPS):
                        v = wy[d][None] * rolled[
                            d, pl.ds(z0 + c, chunk), pl.ds(x0 + t * ELEM, ELEM), :
                        ]
                        acc = v if acc is None else acc + v
                    ysum[c : c + chunk, t * ELEM : (t + 1) * ELEM, :] = acc
            wt = [jnp.broadcast_to(t, (ELEM, size_y)) for t in taps(1, row)]
            for c in range(0, span, chunk):
                acc = None
                for d in range(TAPS):
                    v = wt[d][None] * ysum[c : c + chunk, d : d + ELEM, :]
                    acc = v if acc is None else acc + v
                xsum[c : c + chunk] = acc
            wz = [jnp.broadcast_to(t, (ELEM, size_y)) for t in taps(0, row)]
            warped = None
            for d in range(TAPS):
                v = wz[d][None] * xsum[d : d + ELEM]
                warped = v if warped is None else warped + v
            image = image_ref[pl.ds(z0, ELEM), pl.ds(x0, ELEM), :].astype(f32)
            mismatch = image - warped
            grads = [
                grad_ref[k, pl.ds(z0, ELEM), pl.ds(x0, ELEM), :].astype(f32) for k in range(3)
            ]

            def along_z(volume, weights):
                acc = None
                for i in range(ELEM):
                    v = float(weights[i]) * volume[i]
                    acc = v if acc is None else acc + v
                return acc

            for k in range(3):
                weighted = grads[k] * mismatch
                for a in range(2):
                    plane = along_z(weighted, p[a])
                    for b in range(2):
                        line = jnp.sum(plane * wx_ref[3 + b], axis=0, keepdims=True)
                        vl[(k * 2 + a) * 2 + b, ex, ez : ez + 1, :] = line
            for (k, k2), m in COMP.items():
                product = grads[k] * grads[k2]
                for a in range(3):
                    plane = along_z(product, pairs[a])
                    for b in range(3):
                        line = jnp.sum(plane * wx_ref[b], axis=0, keepdims=True)
                        vs[(m * 3 + a) * 3 + b, ex, ez : ez + 1, :] = line

    def side_by_side(ref, start, count):
        return jnp.concatenate(
            [
                ref[start : start + count, ex].reshape(count * ROWS, size_y)
                for ex in range(count_x)
            ],
            axis=1,
        )

    for m in range(6):
        block = side_by_side(vs, m * 9, 9)
        got = exact_dot(block, bs_ref[...])
        for a in range(3):
            for b in range(3):
                for c in range(3):
                    g = (a * 3 + b) * ROWS
                    stiff_ref[m, a, b, c] = got[g : g + ROWS, c * LANES : (c + 1) * LANES]
    got = exact_dot(side_by_side(vl, 0, 12), bl_ref[...])
    for k in range(3):
        for a in range(2):
            for b in range(2):
                for c in range(2):
                    g = ((k * 2 + a) * 2 + b) * ROWS
                    load_ref[k, a, b, c] = got[g : g + ROWS, c * LANES : (c + 1) * LANES]


def solve_kernel(dims, stiff_ref, load_ref, out_u, out_r, send_x, send_y, got_x, got_y,
                 ssem_x, ssem_y, rsem_x, rsem_y):
    count_x, count_y, stride, nx, ny = dims
    mx, my = lax.axis_index("gx"), lax.axis_index("gy")

    barrier = pltpu.get_barrier_semaphore()
    for d in range(1, nx):
        pl.semaphore_signal(barrier, inc=1, device_id=(lax.rem(mx + d, nx), my), device_id_type=MESH)
    for d in range(1, ny):
        pl.semaphore_signal(barrier, inc=1, device_id=(mx, lax.rem(my + d, ny)), device_id_type=MESH)

    lane = lax.broadcasted_iota(jnp.int32, (ROWS, LANES), 1)
    ix = lane // stride
    iy = lane % stride

    def ones(cond):
        return jnp.where(cond, 1.0, 0.0).astype(jnp.float32)

    def flag(cond):
        return jnp.where(cond, 1.0, 0.0).astype(jnp.float32)

    not_first_x, not_last_x = flag(mx > 0), flag(mx < nx - 1)
    not_first_y, not_last_y = flag(my > 0), flag(my < ny - 1)
    low_x, high_x = ones(ix == 0) * not_first_x, ones(ix == count_x) * not_last_x
    node = ones(ix <= count_x) * ones(iy <= count_y)
    low_y = node * ones(iy == 0) * not_first_y
    high_y = node * ones(iy == count_y) * not_last_y
    owner = node * (1.0 - high_x) * (1.0 - high_y)

    def rolled(v, rows, lanes):
        if rows % ROWS:
            v = pltpu.roll(v, rows % ROWS, 0)
        if lanes % LANES:
            v = pltpu.roll(v, lanes % LANES, 1)
        return v

    sides = [(a, b, c) for a in (0, 1) for b in (0, 1) for c in (0, 1)]

    def scatter(terms):
        out = []
        for k in range(3):
            acc = None
            for a, b, c in sides:
                v = rolled(terms(k, a, b, c), a, b * stride + c)
                acc = v if acc is None else acc + v
            out.append(acc)
        return out

    def stage(rnd, field, tile, axis):
        n, me = (nx, mx) if axis == 0 else (ny, my)
        send, got, ssem, rsem = (
            (send_x, got_x, ssem_x, rsem_x) if axis == 0 else (send_y, got_y, ssem_y, rsem_y)
        )
        for k in range(3):
            send[rnd, k] = field[k]
        send[rnd, 3] = tile if tile is not None else jnp.zeros_like(field[0])
        copies = []
        order = [1, n - 1] + list(range(2, n - 1))
        for d in order:
            near = d in (1, n - 1)
            if tile is None and not near:
                continue
            to = lax.rem(me + d, n)
            target = (to, my) if axis == 0 else (mx, to)
            src = send.at[rnd] if near else send.at[rnd, 3]
            dst = got.at[rnd, d - 1] if near else got.at[rnd, d - 1, 3]
            copy = pltpu.make_async_remote_copy(
                src_ref=src, dst_ref=dst, send_sem=ssem.at[rnd, d - 1],
                recv_sem=rsem.at[rnd, d - 1], device_id=target, device_id_type=MESH,
            )
            copy.start()
            copies.append((d, copy))
        for d, copy in copies:
            copy.wait_recv()
        hop = count_x * stride if axis == 0 else count_y
        low, high = (low_x, high_x) if axis == 0 else (low_y, high_y)
        out = []
        for k in range(3):
            from_low = rolled(got[rnd, 0, k], 0, -hop)
            from_high = rolled(got[rnd, n - 2, k], 0, hop)
            out.append(field[k] + low * from_low + high * from_high)
        if tile is not None:
            for d in range(1, n):
                tile = tile + got[rnd, d - 1, 3]
        return out, tile, [copy for _, copy in copies]

    pending = []

    def exchange(rnd, field, tile):
        field, tile, first = stage(rnd, field, tile, 0)
        field, tile, second = stage(rnd, field, tile, 1)
        pending.extend(first + second)
        return field, tile

    load = scatter(lambda k, a, b, c: load_ref[k, a, b, c])
    pl.semaphore_wait(barrier, nx - 1 + ny - 1)
    r, _ = exchange(0, load, None)
    row = lax.broadcasted_iota(jnp.int32, (ROWS, LANES), 0)
    u = p = q = rr = alpha = None
    for it in range(ITERS):
        force = None
        inputs = {}
        for a, b, c in sides:
            for k2 in range(3):
                v = rolled(r[k2], -a, -(b * stride + c))
                inputs[k2, a, b, c] = v
                block = jnp.stack([
                    stiff_ref[COMP[min(k, k2), max(k, k2)], a : a + 2, b : b + 2, c : c + 2]
                    for k in range(3)
                ])
                term = block * v[None, None, None, None]
                force = term if force is None else force + term
        energy = None
        for (k, a, b, c), v in inputs.items():
            term = force[k, a, b, c] * v
            energy = term if energy is None else energy + term
        square = (r[0] * r[0] + r[1] * r[1] + r[2] * r[2]) * owner
        tile = jnp.where(
            row == 0,
            jnp.sum(square, axis=0, keepdims=True),
            jnp.where(row == 1, jnp.sum(energy, axis=0, keepdims=True), 0.0),
        )
        w, total = exchange(1 + it, scatter(lambda k, a, b, c: force[k, a, b, c]), tile)
        w = [w[k] + RIDGE * r[k] for k in range(3)]
        sums = jnp.sum(total, axis=1, keepdims=True)
        new = sums[0:1]
        image = sums[1:2] + RIDGE * new
        if it == 0:
            p, q = r, w
            alpha = new / image
            u = [alpha * p[k] for k in range(3)]
        else:
            beta = new / rr
            alpha_next = new / (image - beta * new / alpha)
            p = [r[k] + beta * p[k] for k in range(3)]
            q = [w[k] + beta * q[k] for k in range(3)]
            alpha = alpha_next
            u = [u[k] + alpha * p[k] for k in range(3)]
        r = [r[k] - alpha * q[k] for k in range(3)]
        rr = new
    for copy in pending:
        copy.wait_send()
    for k in range(3):
        out_u[k] = u[k]
        out_r[k] = r[k]


def body(nx, ny, reference_image, moving_image, image_gradient, voxel_shift, subvoxel):
    f32 = jnp.float32
    _, count_z, count_x, count_y = voxel_shift.shape
    size_y = count_y * ELEM
    stride = count_y + 8
    padded = padded_2(moving_image, (("gx", 1), ("gy", 2)), HW)
    extra_x = -padded.shape[1] % 8 + (8 if padded.shape[1] % 8 == 0 else 0)
    padded = jnp.pad(padded, ((0, 0), (0, extra_x), (0, 2 * LANES - padded.shape[2])))
    rows = count_z * count_x
    shift = jnp.repeat(voxel_shift.reshape(3, rows, count_y), ELEM, axis=2)
    frac = jnp.repeat(subvoxel.reshape(3, rows, count_y), ELEM, axis=2)
    p = phi()
    pairs = [p[0] * p[0], p[0] * p[1], p[1] * p[1]]
    wx = np.broadcast_to(
        np.stack(pairs + [p[0], p[1]]).astype(np.float32)[:, :, None], (5, ELEM, size_y)
    )
    bs = placed_weights(pairs, count_x, count_y, stride)
    bl = placed_weights([p[0], p[1]], count_x, count_y, stride)
    span = ELEM + TAPS - 1
    vmem = pl.BlockSpec(memory_space=pltpu.VMEM)
    stiff, load = pl.pallas_call(
        functools.partial(element_kernel, (count_z, count_x, size_y)),
        out_shape=[
            jax.ShapeDtypeStruct((6, 3, 3, 3, ROWS, LANES), f32),
            jax.ShapeDtypeStruct((3, 2, 2, 2, ROWS, LANES), f32),
        ],
        in_specs=[vmem] * 8,
        out_specs=[vmem] * 2,
        scratch_shapes=[
            pltpu.VMEM((TAPS, padded.shape[0], padded.shape[1], size_y), f32),
            pltpu.VMEM((span, 3 * ELEM, size_y), f32),
            pltpu.VMEM((span, ELEM, size_y), f32),
            pltpu.VMEM((54, count_x, ROWS, size_y), f32),
            pltpu.VMEM((12, count_x, ROWS, size_y), f32),
        ],
        compiler_params=pltpu.CompilerParams(vmem_limit_bytes=48 * 1024 * 1024),
        name="elements",
    )(padded, reference_image, image_gradient, shift, frac, jnp.asarray(wx), jnp.asarray(bs, jnp.bfloat16),
      jnp.asarray(bl, jnp.bfloat16))
    rounds = ITERS + 1
    dma = pltpu.SemaphoreType.DMA
    u, r = pl.pallas_call(
        functools.partial(solve_kernel, (count_x, count_y, stride, nx, ny)),
        out_shape=[jax.ShapeDtypeStruct((3, ROWS, LANES), f32)] * 2,
        in_specs=[vmem] * 2,
        out_specs=[vmem] * 2,
        scratch_shapes=[
            pltpu.VMEM((rounds, 4, ROWS, LANES), f32),
            pltpu.VMEM((rounds, 4, ROWS, LANES), f32),
            pltpu.VMEM((rounds, nx - 1, 4, ROWS, LANES), f32),
            pltpu.VMEM((rounds, ny - 1, 4, ROWS, LANES), f32),
            dma((rounds, nx - 1)),
            dma((rounds, ny - 1)),
            dma((rounds, nx - 1)),
            dma((rounds, ny - 1)),
        ],
        compiler_params=pltpu.CompilerParams(
            collective_id=0, has_side_effects=True, vmem_limit_bytes=32 * 1024 * 1024
        ),
        name="solve",
    )(stiff, load)

    def unpack(field):
        grid = field[:, : count_z + 1, : count_x * stride]
        return grid.reshape(3, count_z + 1, count_x, stride)[..., :count_y]

    return unpack(u), unpack(r)


def solution(mesh):
    placed = (
        P(None, "gx", "gy"),
        P(None, "gx", "gy"),
        P(None, None, "gx", "gy"),
        P(None, None, "gx", "gy"),
        P(None, None, "gx", "gy"),
    )
    return jax.shard_map(
        functools.partial(body, mesh.shape["gx"], mesh.shape["gy"]),
        mesh=mesh,
        in_specs=placed,
        out_specs=(P(None, None, "gx", "gy"), P(None, None, "gx", "gy")),
        check_vma=False,
    )
```

time: 1550 us -> 82 us (0.05); the launches traced: 1520 us -> 81.6 us
  local copies, waits for them, and re-layouts: 1200 us -> 8.46 us
  blocking collectives: 203 us -> 0 us
  Pallas kernels: 0 us -> 54.1 us
  starting transfers between devices: 46.1 us -> 8.37 us
  waiting for transfers between devices: 33.4 us -> 7.58 us
  other arithmetic: 24.1 us -> 2.32 us
    gather x1070 -> x0, local copies, waits for them, and re-layouts: 1090 us -> none
    psum x5 -> x0, blocking collectives: 203 us -> none  [the longest x3 120 us: squares(): return lax.psum(jnp.sum(residual * residual * owner_weight), ('gx', 'gy'))]
    convert_element_type x16 -> x0, local copies, waits for them, and re-layouts: 83.5 us -> none  [the longest x12 64.1 us: body(): element_major(image_gradient[component], count_z, count_x, count_y)]
    pallas_call x0 -> x2, Pallas kernels: none -> 54.1 us  [the longest x1 35.8 us: body(): pl.pallas_call(functools.partial(solve_kernel, (count_x, count_y, stride,...]
    ppermute x10 -> x2, starting transfers between devices: 32.9 us -> 5.79 us  [padded_2(): lax.ppermute(tail, axis, [(i, (i + 1) % count) for i in range(ends)])]
    ppermute x10 -> x2, waiting for transfers between devices: 31.6 us -> 6.61 us  [padded_2(): lax.ppermute(head, axis, [((i + 1) % count, i) for i in range(ends)])]
  transfers between devices with their start and end apart: 20 -> 4, of which waited for: 12 -> 3; matrix products, arithmetic and copies ran while one was open for 38% -> 3% of each run, Pallas kernels for 0% -> 0%
where the time goes in v1:
time: 82 us; the launch traced here: 81.6 us
  Pallas kernels  54.1 us (66%)
  local copies, waits for them, and re-layouts  8.46 us (10%)
  starting transfers between devices  8.37 us (10%)
  waiting for transfers between devices  7.58 us (9%)
  other arithmetic  2.32 us (3%)
    pallas_call x1, Pallas kernels, body(): pl.pallas_call(functools.partial(solve_kernel, (count_x, count_y, stride,...  35.8 us
    pallas_call x1, Pallas kernels, body(): pl.pallas_call(functools.partial(element_kernel, (count_z, count_x, size_...  18.3 us
    ppermute x2, waiting for transfers between devices, padded_2(): lax.ppermute(head, axis, [((i + 1) % count, i) for i in range(ends)])  6.61 us
    ppermute x2, starting transfers between devices, padded_2(): lax.ppermute(tail, axis, [(i, (i + 1) % count) for i in range(ends)])  5.79 us
    ppermute x2, starting transfers between devices, padded_2(): lax.ppermute(head, axis, [((i + 1) % count, i) for i in range(ends)])  2.59 us
    slice x3, local copies, waits for them, and re-layouts, padded_2(): lax.slice_in_dim(cells, cells.shape[dim] - width, cells.shape[dim], axis=...  2.54 us
    concatenate x2, other arithmetic, padded_2(): jnp.concatenate([lax.ppermute(tail, axis, [(i, (i + 1) % count) for i in...  2.32 us
  transfers between devices with their start and end apart: 4, of which 3 were waited for; matrix products, arithmetic and copies ran while one was open for 3% of the time, Pallas kernels for 0%

profile of v1, /device:TPU:0, one launch (start us, length us, event | category | flops | bytes accessed | tf_op | source)
XLA Modules:
  0.0 81.6 jit_solution(12146020225244102238)
XLA Ops:
  0.6 1.0 %fusion.10 = (f32[44,6,128]{2,1,0:T(8,128)S(1)}, f32[44,6,128]{2,1,0:T(8,128)S(1)}) fusion(f32[44,32,128]{2,1,0:T(8,128)} %param.9), kind=kLoop, calls=%fused_computation.17 | loop fusion | bytes 540672 | tf_op jit(solution)/shard_map/slice | solution.py:53
  1.7 2.4 %collective-permute-start = (f32[44,6,128]{2,1,0:T(8,128)S(1)}, f32[44,6,128]{2,1,0:T(8,128)S(1)}, u32[]{:S(2)}, u32[]{:S(2)}) collective-permute-start(f32[44,6,128]{2,1,0:T(8,128)S(1)} %get-tuple-element.16), channel_id=1, source_target_pairs={{0,8},{8,16},{16,24},{1,9},{9,17},{17,25},{2,10},{10,18},{18,26},{... | collective-permute-start | bytes 405512 | tf_op jit(solution)/shard_map/ppermute | solution.py:56
  4.0 1.3 %collective-permute-start.1 = (f32[44,6,128]{2,1,0:T(8,128)S(1)}, f32[44,6,128]{2,1,0:T(8,128)S(1)}, u32[]{:S(2)}, u32[]{:S(2)}) collective-permute-start(f32[44,6,128]{2,1,0:T(8,128)S(1)} %get-tuple-element.17), channel_id=1, source_target_pairs={{8,0},{16,8},{24,16},{9,1},{17,9},{25,17},{10,2},{18,10},{26,18},{... | collective-permute-start | bytes 405512 | tf_op jit(solution)/shard_map/ppermute | solution.py:58
  5.3 0.8 copy.22
  6.2 0.8 copy.23
  7.0 0.0 collective-permute-done
  7.0 2.5 %collective-permute-done.1 = f32[44,6,128]{2,1,0:T(8,128)S(1)} collective-permute-done((f32[44,6,128]{2,1,0:T(8,128)S(1)}, f32[44,6,128]{2,1,0:T(8,128)S(1)}, u32[]{:S(2)}, u32[]{:S(2)}) %collective-permute-start.1) | collective-permute-done | bytes 135200 | tf_op jit(solution)/shard_map/ppermute | solution.py:58
  9.5 1.2 %pad_maximum_fusion = f32[44,44,128]{2,1,0:T(8,128)S(1)} fusion(f32[44,6,128]{2,1,0:T(8,128)S(1)} %collective-permute-done.1, f32[44,32,128]{2,1,0:T(8,128)} %param.9, f32[44,6,128]{2,1,0:T(8,128)S(1)} %collective-permute-done), kind=kLoop, calls=%fused_computation.13 | loop fusion | flops 495616 | bytes 1982464 | tf_op jit(solution)/shard_map/concatenate | solution.py:54
  10.7 0.3 fusion.9
  11.0 1.2 %copy.18 = f32[44,44,6]{1,0,2:T(8,128)} copy(f32[44,44,6]{2,1,0:T(8,128)S(1)} %get-tuple-element.14) | data formatting | bytes 92928 | tf_op jit(solution)/shard_map/slice | solution.py:53
  12.2 3.4 %collective-permute-start.2 = (f32[44,44,6]{1,0,2:T(8,128)}, f32[44,44,6]{1,0,2:T(8,128)S(1)}, u32[]{:S(2)}, u32[]{:S(2)}) collective-permute-start(f32[44,44,6]{1,0,2:T(8,128)} %copy.18), channel_id=1, source_target_pairs={{0,1},{1,2},{2,3},{3,4},{4,5},{5,6},{6,7},{8,9},{9,10},{10,11},{11... | collective-permute-start | bytes 139400 | tf_op jit(solution)/shard_map/ppermute | solution.py:56
  15.6 0.0 copy-start.4
  15.6 0.5 copy.19
  16.1 1.3 %collective-permute-start.3 = (f32[44,44,6]{1,0,2:T(8,128)S(1)}, f32[44,44,6]{1,0,2:T(8,128)}, u32[]{:S(2)}, u32[]{:S(2)}) collective-permute-start(f32[44,44,6]{1,0,2:T(8,128)S(1)} %copy.19), channel_id=1, source_target_pairs={{1,0},{2,1},{3,2},{4,3},{5,4},{6,5},{7,6},{9,8},{10,9},{11,10},{12... | collective-permute-start | bytes 139400 | tf_op jit(solution)/shard_map/ppermute | solution.py:58
  17.4 0.1 copy.24.shift_ref
  17.5 0.1 copy.25.frac_ref
  17.6 1.0 %collective-permute-done.2 = f32[44,44,6]{1,0,2:T(8,128)S(1)} collective-permute-done((f32[44,44,6]{1,0,2:T(8,128)}, f32[44,44,6]{1,0,2:T(8,128)S(1)}, u32[]{:S(2)}, u32[]{:S(2)}) %collective-permute-start.2) | collective-permute-done | bytes 46496 | tf_op jit(solution)/shard_map/ppermute | solution.py:56
  18.6 0.5 copy.20
  19.1 4.2 %collective-permute-done.3 = f32[44,44,6]{1,0,2:T(8,128)} collective-permute-done((f32[44,44,6]{1,0,2:T(8,128)S(1)}, f32[44,44,6]{1,0,2:T(8,128)}, u32[]{:S(2)}, u32[]{:S(2)}) %collective-permute-start.3) | collective-permute-done | bytes 46496 | tf_op jit(solution)/shard_map/ppermute | solution.py:58
  23.2 1.4 %copy.21 = f32[44,44,6]{2,1,0:T(8,128)S(1)} copy(f32[44,44,6]{1,0,2:T(8,128)} %collective-permute-done.3) | data formatting | bytes 92928 | tf_op jit(solution)/shard_map/ppermute | solution.py:58
  24.7 0.0 copy-done.4
  24.7 0.0 copy-start.5
  24.7 0.0 copy-start
  24.7 0.0 copy-start.1
  24.7 0.0 copy-start.2
  24.7 0.0 copy-start.3
  24.7 1.1 %select_maximum_fusion.pad_ref = f32[44,48,256]{2,1,0:T(8,128)S(1)} fusion(f32[44,44,6]{2,1,0:T(8,128)S(1)} %copy.21, f32[44,44,6]{2,1,0:T(8,128)S(1)} %copy.20, f32[44,6,128]{2,1,0:T(8,128)S(1)} %collective-permute-done.1, f32[44,32,128]{2,1,0:T(8,128)S(1)} %copy-done.4, f32[44,6,128]{2,1,0:T(8,128)S(1)} %collective-permute-done), kind=kLoop, calls=%fused_computation | loop fusion | flops 9191424 | bytes 3246848 | tf_op jit(solution)/shard_map/concatenate | solution.py:54
  25.8 0.0 copy-done.5
  25.8 0.1 jit_solution_.3.wx_ref
  25.9 0.0 copy-done
  25.9 0.0 copy-done.1
  25.9 0.1 copy-done.2
  26.0 0.1 copy-done.3
  26.1 18.3 %elements.1 = (f32[6,3,3,3,8,128]{5,4,3,2,1,0:T(8,128)S(1)}, f32[3,2,2,2,8,128]{5,4,3,2,1,0:T(8,128)S(1)}) custom-call(f32[44,48,256]{2,1,0:T(8,128)S(1)} %select_maximum_fusion.pad_ref, bf16[32,32,128]{2,1,0:T(8,128)(2,1)S(1)} %copy-done.2, bf16[3,32,32,128]{3,2,1,0:T(8,128)(2,1)S(1)} %copy-done, s32[3,16,128]{2,1,0:T(8,128)S(1)} %copy.24.shift_ref, ...), custom_call_target="tpu_custom_call" | custom-call | tf_op jit(solution)/shard_map/elements/pallas_call | solution.py:342
  44.4 35.8 %solve.1 = (f32[3,8,128]{2,1,0:T(8,128)S(1)}, f32[3,8,128]{2,1,0:T(8,128)S(1)}) custom-call(f32[6,3,3,3,8,128]{5,4,3,2,1,0:T(8,128)S(1)} %get-tuple-element.6.stiff_ref, f32[3,2,2,2,8,128]{5,4,3,2,1,0:T(8,128)S(1)} %get-tuple-element.7.load_ref), custom_call_target="tpu_custom_call" | custom-call | tf_op jit(solution)/shard_map/solve/pallas_call | solution.py:363
  80.2 0.1 reshape.26
  80.3 0.6 copy.28
  80.9 0.1 reshape.27
  81.0 0.6 copy.29
  (4 shorter events, 0.0 us)
Async XLA Ops:
  1.7 5.3 %collective-permute-start = (f32[44,6,128]{2,1,0:T(8,128)S(1)}, f32[44,6,128]{2,1,0:T(8,128)S(1)}, u32[]{:S(2)}, u32[]{:S(2)}) collective-permute-start(f32[44,6,128]{2,1,0:T(8,128)S(1)} %get-tuple-element.16), channel_id=1, source_target_pairs={{0,8},{8,16},{16,24},{1,9},{9,17},{17,25},{2,10},{10,18},{18,26},{... | collective-permute-start | bytes 405512 | tf_op jit(solution)/shard_map/ppermute | solution.py:56
  4.0 5.4 %collective-permute-start.1 = (f32[44,6,128]{2,1,0:T(8,128)S(1)}, f32[44,6,128]{2,1,0:T(8,128)S(1)}, u32[]{:S(2)}, u32[]{:S(2)}) collective-permute-start(f32[44,6,128]{2,1,0:T(8,128)S(1)} %get-tuple-element.17), channel_id=1, source_target_pairs={{8,0},{16,8},{24,16},{9,1},{17,9},{25,17},{10,2},{18,10},{26,18},{... | collective-permute-start | bytes 405512 | tf_op jit(solution)/shard_map/ppermute | solution.py:58
  12.2 6.4 %collective-permute-start.2 = (f32[44,44,6]{1,0,2:T(8,128)}, f32[44,44,6]{1,0,2:T(8,128)S(1)}, u32[]{:S(2)}, u32[]{:S(2)}) collective-permute-start(f32[44,44,6]{1,0,2:T(8,128)} %copy.18), channel_id=1, source_target_pairs={{0,1},{1,2},{2,3},{3,4},{4,5},{5,6},{6,7},{8,9},{9,10},{10,11},{11... | collective-permute-start | bytes 139400 | tf_op jit(solution)/shard_map/ppermute | solution.py:56
  15.6 9.1 %copy-start.4 = (f32[44,32,128]{2,1,0:T(8,128)S(1)}, f32[44,32,128]{2,1,0:T(8,128)}, u32[]{:S(2)}) copy-start(f32[44,32,128]{2,1,0:T(8,128)} %param.9) | copy-start | bytes 2162692
  16.1 7.1 %collective-permute-start.3 = (f32[44,44,6]{1,0,2:T(8,128)S(1)}, f32[44,44,6]{1,0,2:T(8,128)}, u32[]{:S(2)}, u32[]{:S(2)}) collective-permute-start(f32[44,44,6]{1,0,2:T(8,128)S(1)} %copy.19), channel_id=1, source_target_pairs={{1,0},{2,1},{3,2},{4,3},{5,4},{6,5},{7,6},{9,8},{10,9},{11,10},{12... | collective-permute-start | bytes 139400 | tf_op jit(solution)/shard_map/ppermute | solution.py:58
  24.7 1.2 %copy-start.5 = (f32[5,8]{1,0:T(8,128)S(1)}, f32[5,8]{1,0:T(8,128)}, u32[]{:S(2)}) copy-start(f32[5,8]{1,0:T(8,128)} %constant.9.clone) | copy-start | bytes 484
  24.7 1.2 %copy-start = (bf16[3,32,32,128]{3,2,1,0:T(8,128)(2,1)S(1)}, bf16[3,32,32,128]{3,2,1,0:T(8,128)(2,1)}, u32[]{:S(2)}) copy-start(bf16[3,32,32,128]{3,2,1,0:T(8,128)(2,1)} %grad_ref.1) | copy-start | bytes 2359300
  24.7 1.2 %copy-start.1 = (bf16[512,384]{1,0:T(8,128)(2,1)S(1)}, bf16[512,384]{1,0:T(8,128)(2,1)}, u32[]{:S(2)}) copy-start(bf16[512,384]{1,0:T(8,128)(2,1)} %constant.10.clone.bs_ref) | copy-start | bytes 1179652
  24.7 1.3 %copy-start.2 = (bf16[32,32,128]{2,1,0:T(8,128)(2,1)S(1)}, bf16[32,32,128]{2,1,0:T(8,128)(2,1)}, u32[]{:S(2)}) copy-start(bf16[32,32,128]{2,1,0:T(8,128)(2,1)} %image_ref.1) | copy-start | bytes 786436
  24.7 1.4 %copy-start.3 = (bf16[512,256]{1,0:T(8,128)(2,1)S(1)}, bf16[512,256]{1,0:T(8,128)(2,1)}, u32[]{:S(2)}) copy-start(bf16[512,256]{1,0:T(8,128)(2,1)} %constant.11.clone.bl_ref) | copy-start | bytes 786436
